TPU v7x, 32 devices: a whole 2x2x4 slice. The times are simulated.
32 devices in a mesh: tm: 8 (over z, y), space: 4 (over x, core).
Axes of the slice: x: 2, y: 2, z: 4, core: 2. Of those that a mesh axis runs over, the one named last changes fastest.
Arguments:
- snapshots: bfloat16 [4096, 3, 4096], P('tm', None, 'space'), may hold values from -6 to 6
- cell_weights: float32 [4096], P('space'), may hold values from 0.25 to 4
- triads: int32 [64, 3], replicated, may hold values from 0 to 127, as said below
- owner_slots: int32 [8, 16], replicated, may hold values from -1 to 63, as said below
Outputs:
- bispectra: float32 [128, 512], P(('tm', 'space'))
Inputs may be any that keep to these rules, and one draw needn't show every extreme that they name: `triads`: every row is (k, l, k + l); all three entries are below 128. `owner_slots`: every triad index stands in exactly one slot of the table; in each row the used slots come first and the others hold -1; some owner fills all 16 slots.
All inputs are finite; a program needn't handle non-finite values.
Results may differ from a plain program's by a relative error of at most 0.0076.
Values may be sent and summed in bfloat16 or wider, within the bound.
A program may use at most 64 MiB of HBM per device.

v0:
```python
import math
import jax
import jax.numpy as jnp
from jax import lax
from jax.sharding import PartitionSpec as P

NB = 16
NT = 256
K = 128


def spectral_table():
    sample = jnp.arange(NT, dtype=jnp.int32)
    freq_bins = jnp.arange(K, dtype=jnp.int32)
    phase_idx = freq_bins[:, None] * sample[None, :] % NT
    angles = 2.0 * math.pi / NT * phase_idx.astype(jnp.float32)
    window = 0.5 - 0.5 * jnp.cos(2.0 * math.pi / NT * sample.astype(jnp.float32))
    norm_scale = math.sqrt(8.0 / (3.0 * NT))
    real_rows = norm_scale * window[None, :] * jnp.cos(angles)
    imag_rows = -norm_scale * window[None, :] * jnp.sin(angles)
    return jnp.stack([real_rows, imag_rows], axis=1).reshape(2 * K, NT).astype(jnp.bfloat16)


def transform(piece):
    snap_total, item_count, cell_count = piece.shape
    blocks = piece.reshape(NB, NT, item_count * cell_count)
    spectra = jnp.einsum(
        "jn,bnc->jbc", spectral_table(), blocks, preferred_element_type=jnp.float32
    )
    return spectra.astype(jnp.bfloat16).reshape(K, 2, NB, item_count, cell_count)


def triad_terms(spectra, weight_rows, triads, triad_index):
    count = triad_index.shape[0]
    lane_total = weight_rows.shape[0]
    triad_freqs = jnp.take(triads, triad_index, axis=0)
    first_spec = (
        jnp.take(spectra, triad_freqs[:, 0], axis=0)
        .reshape(count, 2, NB, lane_total)
        .astype(jnp.float32)
    )
    second_spec = (
        jnp.take(spectra, triad_freqs[:, 1], axis=0)
        .reshape(count, 2, NB, lane_total)
        .astype(jnp.float32)
    )
    third_spec = jnp.take(spectra, triad_freqs[:, 2], axis=0).reshape(count, 2, NB, lane_total)
    prod_real = (
        first_spec[:, 0] * second_spec[:, 0] - first_spec[:, 1] * second_spec[:, 1]
    ) * weight_rows
    prod_imag = (
        first_spec[:, 0] * second_spec[:, 1] + first_spec[:, 1] * second_spec[:, 0]
    ) * weight_rows
    product = jnp.stack([prod_real, prod_imag], axis=1).astype(jnp.bfloat16)
    gram = jnp.einsum("trbc,tsdc->trbsd", product, third_spec, preferred_element_type=jnp.float32)
    bis_real = gram[:, 0, :, 0, :] + gram[:, 1, :, 1, :]
    bis_imag = gram[:, 0, :, 1, :] - gram[:, 1, :, 0, :]
    return jnp.stack([bis_real, bis_imag], axis=1).reshape(count, 2 * NB * NB)


def block_size(amount, quantum):
    return quantum * math.gcd(amount // quantum, max(1, 64 // quantum))


def blocked(index_list, quantum, spectra, weight_rows, triads):
    amount = index_list.shape[0]
    width_blk = block_size(amount, quantum)
    grouped = index_list.reshape(amount // width_blk, width_blk)

    def group_terms(slot_group):
        filled = (slot_group >= 0).astype(jnp.float32)
        return (
            triad_terms(spectra, weight_rows, triads, jnp.maximum(slot_group, 0)) * filled[:, None]
        )

    return lax.map(group_terms, grouped).reshape(amount, 2 * NB * NB)


def shards(snapshots, cell_weights, triads, owner_slots):
    spectra = transform(lax.all_to_all(snapshots, "tm", split_axis=2, concat_axis=0, tiled=True))
    cell_count = spectra.shape[4]
    spectra = spectra.reshape(K, 2 * NB * 3 * cell_count)
    tm_total = lax.axis_size("tm")
    space_total = lax.axis_size("space")
    device_total = tm_total * space_total
    weight_scale = 1.0 / math.sqrt(3.0 * cell_count * device_total)
    local_w = (
        lax.dynamic_slice_in_dim(cell_weights, lax.axis_index("tm") * cell_count, cell_count, 0)
        * weight_scale
    )
    weight_rows = jnp.tile(local_w, 3)
    flat_slots = owner_slots.reshape(-1)
    my_rows = flat_slots.shape[0] // device_total
    return lax.psum_scatter(
        blocked(flat_slots, my_rows, spectra, weight_rows, triads),
        ("tm", "space"),
        scatter_dimension=0,
        tiled=True,
    )


def solution(mesh):
    placed = (P("tm", None, "space"), P("space"), P(), P())
    return jax.shard_map(
        shards, mesh=mesh, in_specs=placed, out_specs=P(("tm", "space"), None), check_vma=False
    )
```

profile of v0, /device:TPU:0, one launch (start us, length us, event | category | flops | bytes accessed | tf_op | source)
XLA Modules:
  0.0 327.5 jit_solution(2348501136595664732)
XLA Ops:
  6.5 7.7 %copy.36 = bf16[512,3,1024]{0,1,2:T(4,128)(2,1)} copy(bf16[512,3,1024]{2,0,1:T(8,128)(2,1)} %param.8) | data formatting | bytes 6291456 | tf_op args[0]
  14.2 7.4 %all-to-all-start = ((bf16[512,3,1024]{0,1,2:T(4,128)(2,1)}), bf16[512,3,1024]{0,1,2:T(4,128)(2,1)}, u32[]{:S(2)}, u32[]{:S(2)}) async-start(bf16[512,3,1024]{0,1,2:T(4,128)(2,1)} %copy.36), calls=%async_computation | async-start | bytes 8388608 | tf_op jit(solution)/shard_map/all_to_all | solution.py:80
  23.5 91.4 %all-to-all-done = bf16[512,3,1024]{0,1,2:T(4,128)(2,1)} async-done(((bf16[512,3,1024]{0,1,2:T(4,128)(2,1)}), bf16[512,3,1024]{0,1,2:T(4,128)(2,1)}, u32[]{:S(2)}, u32[]{:S(2)}) %all-to-all-start) | async-done | bytes 3145760 | tf_op jit(solution)/shard_map/all_to_all | solution.py:80
  114.9 4.5 %copy.54 = bf16[512,3,8,128]{0,2,3,1:T(8,128)(2,1)S(1)} copy(bf16[512,3,8,128]{0,1,3,2:T(4,128)(2,1)} %bitcast) | data formatting | bytes 6291456 | tf_op jit(solution)/shard_map/all_to_all | solution.py:80
  119.4 3.4 %reshape.253 = bf16[16,256,384]{1,0,2:T(8,128)(2,1)} reshape(bf16[8,512,3,128]{1,0,3,2:T(8,128)(2,1)S(1)} %bitcast.74) | data formatting | bytes 6291456 | tf_op jit(solution)/shard_map/reshape | solution.py:26
  122.7 4.2 %fusion.12 = bf16[256,16,384]{2,0,1:T(8,128)(2,1)S(1)} fusion(bf16[256,256,1]{1,0,2:T(8,128)(2,1)S(1)} %reshape.310, bf16[16,256,384]{1,0,2:T(8,128)(2,1)} %reshape.253), kind=kOutput, calls=%fused_computation.46 | convolution fusion | flops 806879232 | bytes 6422528 | tf_op jit(solution)/shard_map/jn,bnc->jbc/dot_general | solution.py:27
  127.0 3.5 %copy.39 = bf16[256,16,384]{2,1,0:T(8,128)(2,1)} copy(bf16[256,16,384]{2,0,1:T(8,128)(2,1)S(1)} %fusion.12) | data formatting | bytes 6291456 | tf_op jit(solution)/shard_map/convert_element_type | solution.py:30
  130.5 4.2 %reshape_reshape.7 = bf16[128,12288]{1,0:T(8,128)(2,1)S(1)} reshape(bf16[256,16,384]{2,1,0:T(8,128)(2,1)} %copy.39) | data formatting | bytes 6291456 | tf_op jit(solution)/shard_map/reshape;reshape | solution.py:82
  134.7 60.4 %while.11 = (s32[]{:T(128)}, f32[2,64,512]{2,1,0:T(8,128)}, s32[2,64]{1,0:T(2,128)S(1)}, s32[64,3]{1,0:T(8,128)S(1)}, bf16[128,12288]{1,0:T(8,128)(2,1)S(1)}, /*index=5*/f32[128]{0:T(128)S(1)}, s32[]{:T(128)}) while((s32[]{:T(128)}, f32[2,64,512]{2,1,0:T(8,128)}, s32[2,64]{1,0:T(2,128)S(1)}, s32[64,3]{1,0:T(8,128)S(1)}, ...), condition=%wide.region_1.3_spmd.clone, body=%wide.region_0.2_spmd.clone.sunk | while | flops 61446336 | bytes 69630632 | solution.py:76
  135.7 2.7 gather_fusion.1
  138.4 1.7 select_convert_fusion.4
  140.0 2.2 copy.61
  142.3 2.7 gather_fusion.2
  145.0 1.7 select_convert_fusion.5
  147.2 1.3 copy-done
  148.5 1.7 multiply_convert_fusion.5
  150.2 2.7 gather_fusion.3
  152.9 1.6 broadcast_select_fusion.5
  155.9 2.9 fusion.30
  163.4 1.6 constant_dynamic-update-slice_fusion.2
  165.9 2.7 gather_fusion.1
  168.6 1.7 select_convert_fusion.4
  170.2 2.2 copy.61
  172.5 2.7 gather_fusion.2
  175.2 1.7 select_convert_fusion.5
  178.7 1.7 multiply_convert_fusion.5
  180.4 2.7 gather_fusion.3
  183.1 1.6 broadcast_select_fusion.5
  186.1 2.9 fusion.30
  193.6 1.6 constant_dynamic-update-slice_fusion.2
  195.1 124.2 %all-reduce.3.cloned.1.call-done = f32[128,512]{1,0:T(8,128)} async-done(((f32[128,512]{1,0:T(8,128)}), f32[128,512]{1,0:T(8,128)}) %all-reduce.3.cloned.1.call-update) | async-done | bytes 262160
  319.4 1.3 constant_dynamic-slice_fusion.1
  (71 shorter events, 17.8 us)
Async XLA Ops:
  14.2 8.4 %copy-start.4 = (s32[64,3]{0,1:T(4,128)S(1)}, s32[64,3]{0,1:T(4,128)}, u32[]{:S(2)}) copy-start(s32[64,3]{0,1:T(4,128)} %param.10) | copy-start | bytes 2308
  14.2 8.5 %copy-start.3 = (s32[8,16]{1,0:T(8,128)S(1)}, s32[8,16]{1,0:T(8,128)}, u32[]{:S(2)}) copy-start(s32[8,16]{1,0:T(8,128)} %param.11) | copy-start | bytes 1540
  14.2 100.7 %all-to-all-start = ((bf16[512,3,1024]{0,1,2:T(4,128)(2,1)}), bf16[512,3,1024]{0,1,2:T(4,128)(2,1)}, u32[]{:S(2)}, u32[]{:S(2)}) async-start(bf16[512,3,1024]{0,1,2:T(4,128)(2,1)} %copy.36), calls=%async_computation | async-start | bytes 8388608 | tf_op jit(solution)/shard_map/all_to_all | solution.py:80
  21.6 297.7 %all-reduce.3.cloned.1.call-start = ((), (), s32[]{:S(2)}) async-start(), calls=%async_computation.1 | async-start | bytes 524288
  146.6 1.9 copy-start
  154.5 1.1 copy-start.1
  154.5 1.4 copy-start.2
  176.8 1.9 copy-start
  184.7 1.1 copy-start.1
  184.8 1.4 copy-start.2
Sparse Core Ops, SparseCore 0:
  195.3 124.0 all-reduce.2
where the time goes:
time: 329 us; the launch traced here: 328 us
  waiting for transfers between devices  216 us (66%)
  local copies, waits for them, and re-layouts  63.2 us (19%)
  other arithmetic  17.4 us (5%)
  between operations  13.5 us (4%)
  matrix products  10.1 us (3%)
  starting transfers between devices  7.45 us (2%)
    unnamed x2, waiting for transfers between devices  124 us
    all_to_all x1, waiting for transfers between devices, shards(): lax.all_to_all(snapshots, 'tm', split_axis=2, concat_axis=0, tiled=True)  91.4 us
    while x18, local copies, waits for them, and re-layouts  10.8 us
    unnamed x7, local copies, waits for them, and re-layouts  9.08 us
    all_to_all x1, starting transfers between devices, shards(): lax.all_to_all(snapshots, 'tm', split_axis=2, concat_axis=0, tiled=True)  7.41 us
  transfers between devices with their start and end apart: 2, of which 2 were waited for; matrix products, arithmetic and copies ran while one was open for 1% of the time, Pallas kernels for 0%

commit v1 on v0

--- a/solution.py
+++ b/solution.py
@@ -7,6 +7,29 @@
 NB = 16
 NT = 256
 K = 128
+
+
+def cut_along(array, dim, peers):
+    dims = array.shape
+    tiles = array.reshape(*dims[:dim], peers, dims[dim] // peers, *dims[dim + 1 :])
+    return jnp.moveaxis(tiles, dim, 0)
+
+
+def joined_along(tiles, dim):
+    tiles = jnp.moveaxis(tiles, 0, dim)
+    lengths = tiles.shape
+    return tiles.reshape(*lengths[:dim], lengths[dim] * lengths[dim + 1], *lengths[dim + 2 :])
+
+
+def exchange_directly(array, axis, split_dim, concat_dim):
+    size, place = (lax.axis_size(axis), lax.axis_index(axis))
+    tiles = cut_along(array, split_dim, size)
+    outs = [tiles[place]]
+    for step in range(1, size):
+        sent = tiles[(place + step) % size]
+        outs.append(lax.ppermute(sent, axis, [(i, (i + step) % size) for i in range(size)]))
+    tiles = jnp.stack(outs)[(place - jnp.arange(size)) % size]
+    return joined_along(tiles, concat_dim)
 
 
 def spectral_table():
@@ -77,7 +100,7 @@
 
 
 def shards(snapshots, cell_weights, triads, owner_slots):
-    spectra = transform(lax.all_to_all(snapshots, "tm", split_axis=2, concat_axis=0, tiled=True))
+    spectra = transform(exchange_directly(snapshots, "tm", 2, 0))
     cell_count = spectra.shape[4]
     spectra = spectra.reshape(K, 2 * NB * 3 * cell_count)
     tm_total = lax.axis_size("tm")

time: 329 us -> 308 us (0.936)
  waiting for transfers between devices: 216 us -> 171 us
  local copies, waits for them, and re-layouts: 63.2 us -> 82.2 us
  starting transfers between devices: 7.45 us -> 16.2 us
    all_to_all x1 -> x0, waiting for transfers between devices: 91.4 us -> none  [shards(): lax.all_to_all(snapshots, 'tm', split_axis=2, concat_axis=0, tiled=True)]
    ppermute x0 -> x7, waiting for transfers between devices: none -> 25.2 us  [exchange_directly(): lax.ppermute(sent, axis, [(i, (i + step) % size) for i in range(size)])]
    another operation x0 -> x12, local copies, waits for them, and re-layouts: none -> 22 us  [the longest x2 12.3 us: transform(): blocks = piece.reshape(NB, NT, item_count * cell_count)]
    unnamed x2, waiting for transfers between devices: 124 us -> 145 us
    ppermute x0 -> x7, starting transfers between devices: none -> 16.2 us  [exchange_directly(): lax.ppermute(sent, axis, [(i, (i + step) % size) for i in range(size)])]
    all_to_all x1 -> x0, starting transfers between devices: 7.41 us -> none  [shards(): lax.all_to_all(snapshots, 'tm', split_axis=2, concat_axis=0, tiled=True)]
    all_to_all x1 -> x0, local copies, waits for them, and re-layouts: 4.48 us -> none  [shards(): lax.all_to_all(snapshots, 'tm', split_axis=2, concat_axis=0, tiled=True)]
    unnamed x7 -> x20, local copies, waits for them, and re-layouts: 9.08 us -> 13 us
  transfers between devices with their start and end apart: 2 -> 8, of which waited for: 2 -> 4; matrix products, arithmetic and copies ran while one was open for 1% -> 5% of each run, Pallas kernels for 0% -> 0%
where the time goes in v1:
time: 308 us; the launch traced here: 307 us
  waiting for transfers between devices  171 us (56%)
  local copies, waits for them, and re-layouts  82.2 us (27%)
  other arithmetic  17.6 us (6%)
  starting transfers between devices  16.2 us (5%)
  between operations  13.6 us (4%)
  matrix products  6.88 us (2%)
    unnamed x2, waiting for transfers between devices  145 us
    ppermute x7, waiting for transfers between devices, exchange_directly(): lax.ppermute(sent, axis, [(i, (i + step) % size) for i in range(size)])  25.2 us
    ppermute x7, starting transfers between devices, exchange_directly(): lax.ppermute(sent, axis, [(i, (i + step) % size) for i in range(size)])  16.2 us
    unnamed x20, local copies, waits for them, and re-layouts  13 us
    another operation x2, local copies, waits for them, and re-layouts, transform(): blocks = piece.reshape(NB, NT, item_count * cell_count)  12.3 us
    another operation x9, local copies, waits for them, and re-layouts  8.86 us
    while x18, local copies, waits for them, and re-layouts  8.66 us
  transfers between devices with their start and end apart: 8, of which 4 were waited for; matrix products, arithmetic and copies ran while one was open for 5% of the time, Pallas kernels for 0%

profile of v1, /device:TPU:0, one launch (start us, length us, event | category | flops | bytes accessed | tf_op | source)
XLA Modules:
  0.0 307.3 jit_solution(1680732654775428275)
XLA Ops:
  6.5 3.2 %copy.68 = bf16[512,3,1024]{0,2,1:T(8,128)(2,1)S(1)} copy(bf16[512,3,1024]{2,0,1:T(8,128)(2,1)} %param.8) | data formatting | bytes 6291456 | tf_op args[0]
  11.4 2.0 copy.70
  13.4 3.0 collective-permute-start
  16.3 1.9 copy.71
  21.1 2.6 collective-permute-start.2
  26.4 2.7 collective-permute-start.4
  33.9 1.8 bitcast_dynamic-update-slice_fusion.6
  35.6 3.7 %collective-permute-start.6 = (bf16[512,3,128]{2,0,1:T(8,128)(2,1)S(1)}, bf16[512,3,128]{2,0,1:T(8,128)(2,1)S(1)}, u32[]{:S(2)}, u32[]{:S(2)}) collective-permute-start(bf16[512,3,128]{2,0,1:T(8,128)(2,1)S(1)} %bitcast.97), channel_id=1, source_target_pairs={{0,28},{4,0},{8,4},{12,8},{16,12},{20,16},{24,20},{28,24},{1,29},{... | collective-permute-start | bytes 1179656 | tf_op jit(solution)/shard_map/ppermute | solution.py:30
  39.3 1.8 bitcast_dynamic-update-slice_fusion.5
  41.1 21.6 %collective-permute-done.2 = bf16[512,3,128]{2,0,1:T(8,128)(2,1)} collective-permute-done((bf16[512,3,128]{2,0,1:T(8,128)(2,1)S(1)}, bf16[512,3,128]{2,0,1:T(8,128)(2,1)}, u32[]{:S(2)}, u32[]{:S(2)}) %collective-permute-start.2) | collective-permute-done | bytes 393248 | tf_op jit(solution)/shard_map/ppermute | solution.py:30
  62.7 1.8 bitcast_dynamic-update-slice_fusion.4
  67.1 3.3 %collective-permute-done.6 = bf16[512,3,128]{2,0,1:T(8,128)(2,1)S(1)} collective-permute-done((bf16[512,3,128]{2,0,1:T(8,128)(2,1)S(1)}, bf16[512,3,128]{2,0,1:T(8,128)(2,1)S(1)}, u32[]{:S(2)}, u32[]{:S(2)}) %collective-permute-start.6) | collective-permute-done | bytes 393248 | tf_op jit(solution)/shard_map/ppermute | solution.py:30
  71.1 3.0 gather_fusion.4
  74.2 4.7 %copy.84 = bf16[8,512,3,128]{3,2,1,0:T(4,128)(2,1)} copy(bf16[8,512,3,128]{3,1,2,0:T(8,128)(2,1)S(1)} %gather_fusion.4) | data formatting | bytes 6291456 | tf_op jit(solution)/shard_map/reshape;reshape | solution.py:49
  78.8 7.7 %reshape.383 = bf16[16,256,384]{2,1,0:T(8,128)(2,1)S(1)} reshape(bf16[8,512,3,128]{3,2,1,0:T(4,128)(2,1)} %copy.84) | data formatting | bytes 6291456 | tf_op jit(solution)/shard_map/reshape;reshape | solution.py:49
  87.5 3.5 %copy.79 = bf16[256,16,384]{2,1,0:T(8,128)(2,1)} copy(bf16[256,16,384]{2,0,1:T(8,128)(2,1)S(1)} %convolution_convert_fusion) | data formatting | bytes 6291456 | tf_op jit(solution)/shard_map/convert_element_type | solution.py:53
  91.0 4.2 %reshape_reshape.11 = bf16[128,12288]{1,0:T(8,128)(2,1)S(1)} reshape(bf16[256,16,384]{2,1,0:T(8,128)(2,1)} %copy.79) | data formatting | bytes 6291456 | tf_op jit(solution)/shard_map/reshape;reshape | solution.py:105
  95.2 58.5 %while.11 = (s32[]{:T(128)}, f32[2,64,512]{2,1,0:T(8,128)}, s32[2,64]{1,0:T(2,128)S(1)}, s32[64,3]{1,0:T(8,128)S(1)}, bf16[128,12288]{1,0:T(8,128)(2,1)S(1)}, /*index=5*/f32[128]{0:T(128)S(1)}, s32[]{:T(128)}) while((s32[]{:T(128)}, f32[2,64,512]{2,1,0:T(8,128)}, s32[2,64]{1,0:T(2,128)S(1)}, s32[64,3]{1,0:T(8,128)S(1)}, ...), condition=%wide.region_1.3_spmd.clone, body=%wide.region_0.2_spmd.clone.sunk | while | flops 61446336 | bytes 69630632 | solution.py:99
  96.2 2.7 gather_fusion.1
  98.9 1.7 select_convert_fusion.4
  100.5 2.2 copy.97
  102.8 2.7 gather_fusion.2
  110.7 2.7 gather_fusion.3
  113.4 1.7 broadcast_select_fusion.5
  115.4 2.9 fusion.28
  125.4 2.7 gather_fusion.1
  129.8 2.2 copy.97
  132.0 2.7 gather_fusion.2
  139.9 2.7 gather_fusion.3
  142.6 1.7 broadcast_select_fusion.5
  144.7 2.9 fusion.28
  153.7 145.5 %all-reduce.3.cloned.1.call-done = f32[128,512]{1,0:T(8,128)} async-done(((f32[128,512]{1,0:T(8,128)}), f32[128,512]{1,0:T(8,128)}) %all-reduce.3.cloned.1.call-update) | async-done | bytes 262160
  (109 shorter events, 44.2 us)
Async XLA Ops:
  6.5 292.6 %all-reduce.3.cloned.1.call-start = ((), (), s32[]{:S(2)}) async-start(), calls=%async_computation | async-start | bytes 524288
  11.4 14.9 %copy-start.5 = (bf16[512,3,1,128]{0,3,2,1:T(8,128)(2,1)S(1)}, bf16[512,3,1,128]{0,3,2,1:T(8,128)(2,1)}, u32[]{:S(2)}) copy-start(bf16[512,3,1,128]{0,3,2,1:T(8,128)(2,1)} %get-tuple-element.117) | copy-start | bytes 1179652
  11.4 17.9 %copy-start.4 = (bf16[512,3,1,128]{0,3,2,1:T(8,128)(2,1)S(1)}, bf16[512,3,1,128]{0,3,2,1:T(8,128)(2,1)}, u32[]{:S(2)}) copy-start(bf16[512,3,1,128]{0,3,2,1:T(8,128)(2,1)} %get-tuple-element.122) | copy-start | bytes 1179652
  11.4 20.2 %copy-start.3 = (bf16[512,3,1,128]{0,3,2,1:T(8,128)(2,1)S(1)}, bf16[512,3,1,128]{0,3,2,1:T(8,128)(2,1)}, u32[]{:S(2)}) copy-start(bf16[512,3,1,128]{0,3,2,1:T(8,128)(2,1)} %get-tuple-element.116) | copy-start | bytes 1179652
  13.4 19.1 %collective-permute-start = (bf16[512,3,128]{2,0,1:T(8,128)(2,1)}, bf16[512,3,128]{2,0,1:T(8,128)(2,1)}, u32[]{:S(2)}, u32[]{:S(2)}) collective-permute-start(bf16[512,3,128]{2,0,1:T(8,128)(2,1)} %bitcast.2), channel_id=1, source_target_pairs={{0,4},{4,8},{8,12},{12,16},{16,20},{20,24},{24,28},{28,0},{1,5},{5... | collective-permute-start | bytes 1179656 | tf_op jit(solution)/shard_map/ppermute | solution.py:30
  18.3 17.4 %collective-permute-start.1 = (bf16[512,3,128]{2,0,1:T(8,128)(2,1)}, bf16[512,3,128]{2,0,1:T(8,128)(2,1)}, u32[]{:S(2)}, u32[]{:S(2)}) collective-permute-start(bf16[512,3,128]{2,0,1:T(8,128)(2,1)} %bitcast.4), channel_id=1, source_target_pairs={{0,8},{4,12},{8,16},{12,20},{16,24},{20,28},{24,0},{28,4},{1,9},{5... | collective-permute-start | bytes 1179656 | tf_op jit(solution)/shard_map/ppermute | solution.py:30
  19.9 12.4 %copy-start.7 = (s32[64,3]{0,1:T(4,128)S(1)}, s32[64,3]{0,1:T(4,128)}, u32[]{:S(2)}) copy-start(s32[64,3]{0,1:T(4,128)} %param.10) | copy-start | bytes 2308
  19.9 12.5 %copy-start.6 = (s32[8,16]{1,0:T(8,128)S(1)}, s32[8,16]{1,0:T(8,128)}, u32[]{:S(2)}) copy-start(s32[8,16]{1,0:T(8,128)} %param.11) | copy-start | bytes 1540
  21.1 41.5 %collective-permute-start.2 = (bf16[512,3,128]{2,0,1:T(8,128)(2,1)S(1)}, bf16[512,3,128]{2,0,1:T(8,128)(2,1)}, u32[]{:S(2)}, u32[]{:S(2)}) collective-permute-start(bf16[512,3,128]{2,0,1:T(8,128)(2,1)S(1)} %bitcast.96), channel_id=1, source_target_pairs={{0,12},{4,16},{8,20},{12,24},{16,28},{20,0},{24,4},{28,8},{1,13},{... | collective-permute-start | bytes 1179656 | tf_op jit(solution)/shard_map/ppermute | solution.py:30
  24.9 39.9 %collective-permute-start.3 = (bf16[512,3,128]{2,0,1:T(8,128)(2,1)S(1)}, bf16[512,3,128]{2,0,1:T(8,128)(2,1)S(1)}, u32[]{:S(2)}, u32[]{:S(2)}) collective-permute-start(bf16[512,3,128]{2,0,1:T(8,128)(2,1)S(1)} %bitcast.95), channel_id=1, source_target_pairs={{0,16},{4,20},{8,24},{12,28},{16,0},{20,4},{24,8},{28,12},{1,17},{... | collective-permute-start | bytes 1179656 | tf_op jit(solution)/shard_map/ppermute | solution.py:30
  26.4 39.1 %collective-permute-start.4 = (bf16[512,3,128]{2,0,1:T(8,128)(2,1)S(1)}, bf16[512,3,128]{2,0,1:T(8,128)(2,1)S(1)}, u32[]{:S(2)}, u32[]{:S(2)}) collective-permute-start(bf16[512,3,128]{2,0,1:T(8,128)(2,1)S(1)} %bitcast.94), channel_id=1, source_target_pairs={{0,20},{4,24},{8,28},{12,0},{16,4},{20,8},{24,12},{28,16},{1,21},{... | collective-permute-start | bytes 1179656 | tf_op jit(solution)/shard_map/ppermute | solution.py:30
  32.5 33.8 %collective-permute-start.5 = (bf16[512,3,128]{2,0,1:T(8,128)(2,1)S(1)}, bf16[512,3,128]{2,0,1:T(8,128)(2,1)S(1)}, u32[]{:S(2)}, u32[]{:S(2)}) collective-permute-start(bf16[512,3,128]{2,0,1:T(8,128)(2,1)S(1)} %bitcast.98), channel_id=1, source_target_pairs={{0,24},{4,28},{8,0},{12,4},{16,8},{20,12},{24,16},{28,20},{1,25},{... | collective-permute-start | bytes 1179656 | tf_op jit(solution)/shard_map/ppermute | solution.py:30
  35.6 34.7 %collective-permute-start.6 = (bf16[512,3,128]{2,0,1:T(8,128)(2,1)S(1)}, bf16[512,3,128]{2,0,1:T(8,128)(2,1)S(1)}, u32[]{:S(2)}, u32[]{:S(2)}) collective-permute-start(bf16[512,3,128]{2,0,1:T(8,128)(2,1)S(1)} %bitcast.97), channel_id=1, source_target_pairs={{0,28},{4,0},{8,4},{12,8},{16,12},{20,16},{24,20},{28,24},{1,29},{... | collective-permute-start | bytes 1179656 | tf_op jit(solution)/shard_map/ppermute | solution.py:30
  107.1 1.9 copy-start
  113.4 2.0 copy-start.1
  113.4 2.0 copy-start.2
  136.4 1.9 copy-start
  142.6 2.0 copy-start.1
  142.6 2.0 copy-start.2
Sparse Core Ops, SparseCore 0:
  153.8 145.2 all-reduce.2
